TPU v7x, 32 devices: a whole 2x2x4 slice. The times are simulated.
32 devices in a mesh: groups: 2 (over y), lat: 16 (over z, x, core).
Axes of the slice: x: 2, y: 2, z: 4, core: 2. Of those that a mesh axis runs over, the one named last changes fastest.
Arguments:
- grid_lat: bfloat16 [65536, 512], P(('groups', 'lat')), parts along dimension 0, may hold values from -6 to 6
- mesh_lat: bfloat16 [4096, 512], P(('groups', 'lat')), parts along dimension 0, may hold values from -6 to 6
- enc_feat: bfloat16 [4, 131072], P(None, ('groups', 'lat')), parts along dimension 1, may hold values from -5 to 5
- enc_src: int32 [131072], P(('groups', 'lat')), parts along dimension 0, may hold values from 0 to 2047
- enc_dst: int32 [131072], P(('groups', 'lat')), parts along dimension 0, may hold values from 0 to 383, as said below
- mesh_send: int32 [32, 16, 8], P(('groups', 'lat')), parts along dimension 0, may hold values from 0 to 127
- mesh_senders: int32 [65536], P(('groups', 'lat')), parts along dimension 0, may hold values from 0 to 255, as said below
- mesh_recv: int32 [65536], P(('groups', 'lat')), parts along dimension 0, may hold values from 0 to 127
- w_enc_grid: bfloat16 [512, 512], replicated, may hold values from -0.25 to 0.25
- w_enc_feat: bfloat16 [4, 512], replicated, may hold values from -3 to 3
- b_enc: float32 [512], replicated, may hold values from -3 to 3
- w_enc_out: bfloat16 [512, 512], replicated, may hold values from -0.25 to 0.25
- b_enc_out: float32 [512], replicated, may hold values from -3 to 3
- w_node_self: bfloat16 [512, 512], replicated, may hold values from -0.25 to 0.25
- w_node_agg: bfloat16 [512, 512], replicated, may hold values from -0.09375 to 0.09375
- b_node: float32 [512], replicated, may hold values from -3 to 3
- w_node_out: bfloat16 [512, 512], replicated, may hold values from -0.25 to 0.25
- b_node_out: float32 [512], replicated, may hold values from -3 to 3
- gain_node: float32 [512], replicated, may hold values from 0.25 to 1.75
- w_edge_send: bfloat16 [512, 512], replicated, may hold values from -0.25 to 0.25
- w_edge_recv: bfloat16 [512, 512], replicated, may hold values from -0.25 to 0.25
- b_edge: float32 [512], replicated, may hold values from -3 to 3
- w_edge_out: bfloat16 [512, 512], replicated, may hold values from -0.25 to 0.25
- b_edge_out: float32 [512], replicated, may hold values from -1.2 to 1.2
- w_proc_self: bfloat16 [512, 512], replicated, may hold values from -0.25 to 0.25
- w_proc_agg: bfloat16 [512, 512], replicated, may hold values from -0.1875 to 0.1875
- b_proc: float32 [512], replicated, may hold values from -3 to 3
- w_proc_out: bfloat16 [512, 512], replicated, may hold values from -0.25 to 0.25
- b_proc_out: float32 [512], replicated, may hold values from -3 to 3
- gain_proc: float32 [512], replicated, may hold values from 0.25 to 1.75
Outputs:
- mesh_out: bfloat16 [4096, 512], P(('groups', 'lat')), parts along dimension 0
There are 2 independent parts, one for each index of `groups`. A program takes and returns all parts, laid end to end along the dimension named above; an argument that names none is the same for every part. Nothing has to cross between parts.
Inputs may be any that keep to these rules, and one draw needn't show every extreme that they name: `enc_dst`: band 0 has no key below 128 and the last band none at or above 256. `mesh_senders`: on each patch every one of the 128 handed-over slots is the sender of at least one edge.
All inputs are finite; a program needn't handle non-finite values.
Results may differ from a plain program's by a relative error of at most 0.009.
Values may be sent and summed in bfloat16 or wider, within the bound.
A program may use at most 128 MiB of HBM per device.

v0:
```python
import math

import jax
import jax.numpy as jnp
from jax import lax
from jax.sharding import PartitionSpec as P


def extended(block, sides, width):
    for axis, dim in sides:
        count = lax.axis_size(axis)
        forward = [(i, i + 1) for i in range(count - 1)]
        backward = [(target, source) for source, target in forward]
        low = lax.ppermute(
            lax.slice_in_dim(block, block.shape[dim] - width, None, axis=dim), axis, forward
        )
        high = lax.ppermute(lax.slice_in_dim(block, 0, width, axis=dim), axis, backward)
        block = jnp.concatenate([low, block, high], axis=dim)
    return block


def layer_norm(values, gain):
    center = values - jnp.mean(values, -1, keepdims=True)
    spread = jnp.mean(center * center, -1, keepdims=True)
    return center * lax.rsqrt(spread + 1e-05) * gain


def node_update(latent, summed, w_self, w_agg, bias, w_out, b_out, gain):
    preact = (
        jnp.dot(latent, w_self, preferred_element_type=jnp.float32)
        + jnp.dot(summed, w_agg, preferred_element_type=jnp.float32)
        + bias
    )
    hidden = jax.nn.silu(preact).astype(jnp.bfloat16)
    update = jnp.dot(hidden, w_out, preferred_element_type=jnp.float32) + b_out
    return (latent.astype(jnp.float32) + layer_norm(update, gain)).astype(jnp.bfloat16)


def onehot_sum(messages, targets, key_count):
    edge_count = messages.shape[0]
    block_rows = math.gcd(edge_count, 2048)
    labels = jnp.arange(key_count, dtype=jnp.int32)[:, None]

    def add_block(turn, running):
        piece_rows = lax.dynamic_slice_in_dim(messages, turn * block_rows, block_rows, 0)
        piece_targets = lax.dynamic_slice_in_dim(targets, turn * block_rows, block_rows, 0)
        selector = (piece_targets[None, :] == labels).astype(jnp.bfloat16)
        return running + jnp.dot(selector, piece_rows, preferred_element_type=jnp.float32)

    initial = jnp.zeros((key_count, messages.shape[1]), jnp.float32)
    return lax.fori_loop(0, edge_count // block_rows, add_block, initial)


def shards(
    grid_lat,
    mesh_lat,
    enc_feat,
    enc_src,
    enc_dst,
    mesh_send,
    mesh_senders,
    mesh_recv,
    w_enc_grid,
    w_enc_feat,
    b_enc,
    w_enc_out,
    b_enc_out,
    w_node_self,
    w_node_agg,
    b_node,
    w_node_out,
    b_node_out,
    gain_node,
    w_edge_send,
    w_edge_recv,
    b_edge,
    w_edge_out,
    b_edge_out,
    w_proc_self,
    w_proc_agg,
    b_proc,
    w_proc_out,
    b_proc_out,
    gain_proc,
):
    patch_rows = mesh_lat.shape[0]
    latent_width = mesh_lat.shape[1]
    preact = jnp.dot(grid_lat[enc_src], w_enc_grid, preferred_element_type=jnp.float32)
    preact = (
        preact
        + lax.dot_general(
            enc_feat, w_enc_feat, (((0,), (0,)), ((), ())), preferred_element_type=jnp.float32
        )
        + b_enc
    )
    hidden = jax.nn.silu(preact).astype(jnp.bfloat16)
    messages = (jnp.dot(hidden, w_enc_out, preferred_element_type=jnp.float32) + b_enc_out).astype(
        jnp.bfloat16
    )
    partial_sum = (
        onehot_sum(messages, enc_dst, 3 * patch_rows)
        .astype(jnp.bfloat16)
        .reshape(3, patch_rows, latent_width)
    )
    widened = extended(partial_sum, (("lat", 0),), 1).astype(jnp.float32)
    enc_agg = (widened[2] + widened[0] + widened[4]).astype(jnp.bfloat16)
    mesh_mid = node_update(
        mesh_lat, enc_agg, w_node_self, w_node_agg, b_node, w_node_out, b_node_out, gain_node
    )
    handed = lax.all_to_all(mesh_send, "lat", split_axis=1, concat_axis=0, tiled=True)
    peer_count = handed.shape[0]
    everything = lax.all_gather(mesh_mid, "lat", axis=0, tiled=True)
    own_index = lax.axis_index("lat")
    remote_global = (
        jnp.arange(peer_count, dtype=jnp.int32)[:, None] * patch_rows + handed[:, 0, :]
    ).reshape(-1)
    local_global = own_index * patch_rows + jnp.arange(patch_rows, dtype=jnp.int32)
    lookup = jnp.concatenate([local_global, remote_global])
    sender_latent = everything[lookup[mesh_senders]]
    preact = jnp.dot(sender_latent, w_edge_send, preferred_element_type=jnp.float32)
    preact = (
        preact
        + jnp.dot(mesh_mid[mesh_recv], w_edge_recv, preferred_element_type=jnp.float32)
        + b_edge
    )
    hidden = jax.nn.silu(preact).astype(jnp.bfloat16)
    edge_messages = (
        jnp.dot(hidden, w_edge_out, preferred_element_type=jnp.float32) + b_edge_out
    ).astype(jnp.bfloat16)
    proc_agg = onehot_sum(edge_messages, mesh_recv, patch_rows).astype(jnp.bfloat16)
    return node_update(
        mesh_mid, proc_agg, w_proc_self, w_proc_agg, b_proc, w_proc_out, b_proc_out, gain_proc
    )


def solution(mesh):
    placed = (
        P(("groups", "lat"), None),
        P(("groups", "lat"), None),
        P(None, ("groups", "lat")),
        P(("groups", "lat")),
        P(("groups", "lat")),
        P(("groups", "lat"), None, None),
        P(("groups", "lat")),
        P(("groups", "lat")),
        P(),
        P(),
        P(),
        P(),
        P(),
        P(),
        P(),
        P(),
        P(),
        P(),
        P(),
        P(),
        P(),
        P(),
        P(),
        P(),
        P(),
        P(),
        P(),
        P(),
        P(),
        P(),
    )
    return jax.shard_map(
        shards, mesh=mesh, in_specs=placed, out_specs=P(("groups", "lat"), None), check_vma=False
    )
```

profile of v0, /device:TPU:0, one launch (start us, length us, event | category | flops | bytes accessed | tf_op | source)
XLA Modules:
  0.0 137.2 jit_solution(14668512678583220274)
XLA Ops:
  6.5 0.0 copy-start
  6.5 0.0 all-gather.2.cloned.1.call-start
  6.5 0.9 fusion.42
  7.4 0.7 copy-done
  8.1 17.3 %gather_fusion = bf16[4096,512]{1,0:T(8,128)(2,1)} fusion(bf16[2048,512]{1,0:T(8,128)(2,1)S(1)} %copy-done, s32[4096]{0:T(1024)S(1)} %fusion.42), kind=kCustom, calls=%fused_computation | custom fusion | bytes 8404992 | tf_op jit(solution)/shard_map/gather | solution.py:88
  25.5 7.9 %fusion.55 = f32[4096,512]{1,0:T(8,128)} fusion(bf16[4096,512]{1,0:T(8,128)(2,1)} %gather_fusion, bf16[512,512]{1,0:T(8,128)(2,1)} %param.40), kind=kOutput, calls=%fused_computation.73 | convolution fusion | flops 2147483648 | bytes 13107200 | tf_op jit(solution)/shard_map/dot_general | solution.py:88
  33.4 0.0 copy-done.13
  33.4 0.0 copy-done.14
  33.4 0.0 copy-done.15
  33.4 0.0 copy-done.16
  33.4 0.0 copy-start.6
  33.5 8.0 %add_convert_fusion = bf16[4096,512]{1,0:T(8,128)(2,1)} fusion(bf16[512,512]{1,0:T(8,128)(2,1)} %param.43, f32[512]{0:T(512)S(1)} %copy-done.15, f32[4096,512]{1,0:T(8,128)} %fusion.55, bf16[4,4096]{1,0:T(4,128)(2,1)S(1)} %copy-done.13, bf16[4,512]{1,0:T(4,128)(2,1)S(1)} %copy-done.14, f32[512]{0:T(512)S(1)} %copy-done.16), kind=kOutput, calls=%fused_computation.11 | convolution fusion | flops 2183135232 | bytes 13148160 | tf_op jit(solution)/shard_map/dot_general | solution.py:97
  41.5 0.0 copy-done.6
  41.5 0.0 copy-start.18
  41.5 5.4 %while.9 = (s32[]{:T(128)}, f32[384,512]{1,0:T(8,128)S(1)}, s32[4096]{0:T(1024)S(1)}, bf16[4096,512]{1,0:T(8,128)(2,1)}, s32[]{:T(128)}, /*index=5*/s32[]{:T(128)}, s32[]{:T(128)}, s32[]{:T(128)}) while((s32[]{:T(128)}, f32[384,512]{1,0:T(8,128)S(1)}, s32[4096]{0:T(1024)S(1)}, bf16[4096,512]{1,0:T(8,128)(2,1)}, s32[]{:T(128)}, ...), condition=%wide.region_1.2_spmd.clone, body=%wide.region_0.1_spmd.clone.sunk | while | flops 806486016 | bytes 3694741 | solution.py:51
  41.5 2.7 %fusion.81 = f32[384,512]{1,0:T(8,128)S(1)} fusion(bf16[4096,512]{1,0:T(8,128)(2,1)} %get-tuple-element.193, s32[]{:T(128)S(6)} %select_n.46, s32[2048]{0:T(1024)S(1)} %dynamic_slice.27, f32[384,512]{1,0:T(8,128)S(1)} %get-tuple-element.183, pred[]{:T(512)S(6)} %compare.3), kind=kOutput, calls=%fused_computation.9.clone.1 | convolution fusion | flops 806486016 | bytes 3678213 | tf_op jit(solution)/shard_map/while/body/eval_jaxpr/dot_general | solution.py:48
  44.3 2.6 %fusion.81 = f32[384,512]{1,0:T(8,128)S(1)} fusion(bf16[4096,512]{1,0:T(8,128)(2,1)} %get-tuple-element.193, s32[]{:T(128)S(6)} %select_n.46, s32[2048]{0:T(1024)S(1)} %dynamic_slice.27, f32[384,512]{1,0:T(8,128)S(1)} %get-tuple-element.183, pred[]{:T(512)S(6)} %compare.3), kind=kOutput, calls=%fused_computation.9.clone.1 | convolution fusion | flops 806486016 | bytes 3678213 | tf_op jit(solution)/shard_map/while/body/eval_jaxpr/dot_general | solution.py:48
  46.9 0.0 copy-start.10
  46.9 0.0 copy-start.9
  46.9 0.0 copy-start.7
  46.9 0.0 copy-start.8
  47.0 0.1 convert_element_type.53
  47.0 2.4 %collective-permute-start = (bf16[1,128,512]{2,1,0:T(8,128)(2,1)S(1)}, bf16[1,128,512]{2,1,0:T(8,128)(2,1)S(1)}, u32[]{:S(2)}, u32[]{:S(2)}) collective-permute-start(bf16[1,128,512]{2,1,0:T(8,128)(2,1)S(1)} %get-tuple-element.143), channel_id=1, source_target_pairs={{0,1},{1,2},{2,3},{3,4},{4,5},{5,6},{6,7},{7,8},{8,9},{9,10},{10,1... | collective-permute-start | bytes 393224 | tf_op jit(solution)/shard_map/ppermute | solution.py:14
  49.4 1.3 collective-permute-start.1
  50.7 0.0 copy-done.5
  50.7 1.3 fusion.54
  52.0 0.0 collective-permute-done
  52.0 2.7 %collective-permute-done.1 = bf16[1,128,512]{2,1,0:T(8,128)(2,1)S(1)} collective-permute-done((bf16[1,128,512]{2,1,0:T(8,128)(2,1)S(1)}, bf16[1,128,512]{2,1,0:T(8,128)(2,1)S(1)}, u32[]{:S(2)}, u32[]{:S(2)}) %collective-permute-start.1) | collective-permute-done | bytes 131104 | tf_op jit(solution)/shard_map/ppermute | solution.py:17
  54.8 0.0 copy-done.17
  54.8 0.0 copy-done.18
  54.8 1.8 %fusion.50 = (f32[128]{0:T(128)S(1)}, f32[128,512]{1,0:T(8,128)S(1)}) fusion(f32[512]{0:T(512)S(1)} %copy-done.17, bf16[512,512]{1,0:T(8,128)(2,1)} %param.48, f32[128,512]{1,0:T(8,128)S(1)} %fusion.54, bf16[512,512]{1,0:T(8,128)(2,1)} %param.46, bf16[1,128,512]{2,1,0:T(8,128)(2,1)S(1)} %collective-permute-done.1, bf16[3,128,512]{2,1,0:T(8,128)(2,1)S(1)} %bitcast.34, ...), kind=kOutput, calls=%fused_computation.70 | convolution fusion | flops 135593856 | bytes 2232832 | tf_op jit(solution)/shard_map/dot_general | solution.py:35
  56.5 0.2 multiply_reduce_fusion.1
  56.7 0.0 copy-done.10
  56.7 0.8 add_convert_fusion.3
  57.5 0.0 all-gather.2.cloned.1.call-update
  57.6 0.0 copy-done.9
  57.6 0.7 copy.33
  58.2 9.0 %all-to-all-start = ((s32[1,16,8]{2,0,1:T(1,128)}), s32[1,16,8]{2,0,1:T(1,128)S(1)}, u32[]{:S(2)}, u32[]{:S(2)}) async-start(s32[1,16,8]{2,0,1:T(1,128)} %copy.33), calls=%async_computation | async-start | bytes 16384 | tf_op jit(solution)/shard_map/all_to_all | solution.py:110
  67.3 0.0 copy-done.7
  67.3 0.0 copy-done.8
  67.3 0.1 add.229
  67.4 0.1 add.230
  67.5 6.2 %all-to-all-done = s32[1,16,8]{2,0,1:T(1,128)S(1)} async-done(((s32[1,16,8]{2,0,1:T(1,128)}), s32[1,16,8]{2,0,1:T(1,128)S(1)}, u32[]{:S(2)}, u32[]{:S(2)}) %all-to-all-start) | async-done | bytes 544 | tf_op jit(solution)/shard_map/all_to_all | solution.py:110
  73.6 0.5 broadcast.127
  74.1 0.6 reduce.3
  74.7 0.1 squeeze.2
  74.8 0.0 copy-start.1
  74.9 13.1 %gather_fusion.1 = s32[2048]{0:T(1024)S(1)} fusion(s32[256]{0:T(256)S(1)} %pad_add_fusion, s32[2048]{0:T(1024)S(1)} %fusion.43), kind=kCustom, calls=%fused_computation.1 | custom fusion | bytes 24576 | tf_op jit(solution)/shard_map/gather | solution.py:119
  88.0 0.0 copy-start.3
  88.1 9.2 %gather_fusion.3 = bf16[2048,512]{1,0:T(8,128)(2,1)} fusion(bf16[128,512]{1,0:T(8,128)(2,1)S(1)} %copy-done.1, s32[2048]{0:T(1024)S(1)} %fusion.44), kind=kCustom, calls=%fused_computation.3 | custom fusion | bytes 4202496 | tf_op jit(solution)/shard_map/gather | solution.py:123
  97.3 0.2 fusion.56
  97.5 0.0 copy-start.2
  97.5 6.0 %all-gather.2.cloned.1.call-done = bf16[2048,512]{1,0:T(8,128)(2,1)} async-done(((bf16[128,512]{1,0:T(8,128)(2,1)}), bf16[2048,512]{1,0:T(8,128)(2,1)}) %all-gather.2.cloned.1.call-update) | async-done | bytes 2097168 | tf_op jit(solution)/shard_map/all_gather | solution.py:112
  103.5 11.1 %gather_fusion.2 = bf16[2048,512]{1,0:T(8,128)(2,1)} fusion(bf16[2048,512]{1,0:T(8,128)(2,1)} %all-gather.2.cloned.1.call-done, s32[2048]{0:T(1024)S(1)} %broadcast_clamp_fusion), kind=kCustom, calls=%fused_computation.2 | custom fusion | bytes 4202496 | tf_op jit(solution)/shard_map/gather | solution.py:119
  114.6 0.0 copy-done.2
  114.6 4.8 %fusion.57 = f32[2048,512]{1,0:T(8,128)} fusion(bf16[2048,512]{1,0:T(8,128)(2,1)} %gather_fusion.2, bf16[512,512]{1,0:T(8,128)(2,1)S(1)} %copy-done.2), kind=kOutput, calls=%fused_computation.75 | convolution fusion | flops 1073741824 | bytes 6815744 | tf_op jit(solution)/shard_map/dot_general | solution.py:120
  119.4 0.0 copy-done.20
  119.5 0.0 copy-start.11
  119.5 7.2 %add_convert_fusion.1 = bf16[2048,512]{1,0:T(8,128)(2,1)} fusion(bf16[512,512]{1,0:T(8,128)(2,1)} %param.54, f32[512]{0:T(512)S(1)} %copy-done.19, f32[2048,512]{1,0:T(8,128)} %fusion.57, bf16[2048,512]{1,0:T(8,128)(2,1)} %gather_fusion.3, bf16[512,512]{1,0:T(8,128)(2,1)} %param.52, f32[512]{0:T(512)S(1)} %copy-done.20), kind=kOutput, calls=%fused_computation.13 | convolution fusion | flops 2156920832 | bytes 9441280 | tf_op jit(solution)/shard_map/dot_general | solution.py:128
  126.7 2.4 %multiply_convert_fusion.2 = bf16[128,512]{1,0:T(8,128)(2,1)S(1)} fusion(f32[128,512]{1,0:T(8,128)S(1)} %fusion.56, bf16[512,512]{1,0:T(8,128)(2,1)} %param.57, bf16[2048,512]{1,0:T(8,128)(2,1)} %add_convert_fusion.1, s32[2048]{0:T(1024)S(1)} %copy-done.8, f32[512]{0:T(512)S(1)} %copy-done.21), kind=kOutput, calls=%fused_computation.29 | convolution fusion | flops 336330752 | bytes 3024896 | tf_op jit(solution)/shard_map/dot_general | solution.py:31
  129.0 0.3 fusion.53
  129.4 0.2 multiply_reduce_fusion
  129.6 0.0 copy-done.12
  129.6 0.8 add_convert_fusion.2
  (33 shorter events, 0.1 us)
Async XLA Ops:
  6.5 1.6 %copy-start = (bf16[2048,512]{1,0:T(8,128)(2,1)S(1)}, bf16[2048,512]{1,0:T(8,128)(2,1)}, u32[]{:S(2)}) copy-start(bf16[2048,512]{1,0:T(8,128)(2,1)} %param.32) | copy-start | bytes 6291460
  6.5 97.0 %all-gather.2.cloned.1.call-start = ((), (), s32[]{:S(2)}) async-start(), calls=%async_computation.1 | async-start | bytes 2228224 | tf_op jit(solution)/shard_map/all_gather | solution.py:112
  25.5 7.9 %copy-start.13 = (bf16[4,4096]{1,0:T(4,128)(2,1)S(1)}, bf16[4,4096]{1,0:T(4,128)(2,1)}, u32[]{:S(2)}) copy-start(bf16[4,4096]{1,0:T(4,128)(2,1)} %param.34) | copy-start | bytes 98308
  25.5 7.9 %copy-start.14 = (bf16[4,512]{1,0:T(4,128)(2,1)S(1)}, bf16[4,512]{1,0:T(4,128)(2,1)}, u32[]{:S(2)}) copy-start(bf16[4,512]{1,0:T(4,128)(2,1)} %param.41) | copy-start | bytes 12292
  25.5 7.9 %copy-start.15 = (f32[512]{0:T(512)S(1)}, f32[512]{0:T(512)}, u32[]{:S(2)}) copy-start(f32[512]{0:T(512)} %param.44) | copy-start | bytes 6148
  25.5 7.9 %copy-start.16 = (f32[512]{0:T(512)S(1)}, f32[512]{0:T(512)}, u32[]{:S(2)}) copy-start(f32[512]{0:T(512)} %param.42) | copy-start | bytes 6148
  33.4 8.0 %copy-start.6 = (s32[4096]{0:T(1024)S(1)}, s32[4096]{0:T(1024)}, u32[]{:S(2)}) copy-start(s32[4096]{0:T(1024)} %param.36) | copy-start | bytes 49156
  41.5 9.2 %copy-start.5 = (bf16[128,512]{1,0:T(8,128)(2,1)S(1)}, bf16[128,512]{1,0:T(8,128)(2,1)}, u32[]{:S(2)}) copy-start(bf16[128,512]{1,0:T(8,128)(2,1)} %param.33) | copy-start | bytes 393220
  41.5 13.3 %copy-start.17 = (f32[512]{0:T(512)S(1)}, f32[512]{0:T(512)}, u32[]{:S(2)}) copy-start(f32[512]{0:T(512)} %param.49) | copy-start | bytes 6148
  41.5 13.3 %copy-start.18 = (f32[512]{0:T(512)S(1)}, f32[512]{0:T(512)}, u32[]{:S(2)}) copy-start(f32[512]{0:T(512)} %param.47) | copy-start | bytes 6148
  46.9 9.8 %copy-start.10 = (f32[512]{0:T(512)S(1)}, f32[512]{0:T(512)}, u32[]{:S(2)}) copy-start(f32[512]{0:T(512)} %param.50) | copy-start | bytes 6148
  46.9 10.6 %copy-start.9 = (s32[1,16,8]{1,2,0:T(8,128)S(1)}, s32[1,16,8]{1,2,0:T(8,128)}, u32[]{:S(2)}) copy-start(s32[1,16,8]{1,2,0:T(8,128)} %param.37) | copy-start | bytes 1540
  46.9 20.3 %copy-start.7 = (s32[2048]{0:T(1024)S(1)}, s32[2048]{0:T(1024)}, u32[]{:S(2)}) copy-start(s32[2048]{0:T(1024)} %param.38) | copy-start | bytes 24580
  46.9 20.3 %copy-start.8 = (s32[2048]{0:T(1024)S(1)}, s32[2048]{0:T(1024)}, u32[]{:S(2)}) copy-start(s32[2048]{0:T(1024)} %param.39) | copy-start | bytes 24580
  47.0 5.0 %collective-permute-start = (bf16[1,128,512]{2,1,0:T(8,128)(2,1)S(1)}, bf16[1,128,512]{2,1,0:T(8,128)(2,1)S(1)}, u32[]{:S(2)}, u32[]{:S(2)}) collective-permute-start(bf16[1,128,512]{2,1,0:T(8,128)(2,1)S(1)} %get-tuple-element.143), channel_id=1, source_target_pairs={{0,1},{1,2},{2,3},{3,4},{4,5},{5,6},{6,7},{7,8},{8,9},{9,10},{10,1... | collective-permute-start | bytes 393224 | tf_op jit(solution)/shard_map/ppermute | solution.py:14
  49.4 5.3 %collective-permute-start.1 = (bf16[1,128,512]{2,1,0:T(8,128)(2,1)S(1)}, bf16[1,128,512]{2,1,0:T(8,128)(2,1)S(1)}, u32[]{:S(2)}, u32[]{:S(2)}) collective-permute-start(bf16[1,128,512]{2,1,0:T(8,128)(2,1)S(1)} %get-tuple-element.144), channel_id=1, source_target_pairs={{1,0},{2,1},{3,2},{4,3},{5,4},{6,5},{7,6},{8,7},{9,8},{10,9},{11,1... | collective-permute-start | bytes 393224 | tf_op jit(solution)/shard_map/ppermute | solution.py:17
  58.2 15.4 %all-to-all-start = ((s32[1,16,8]{2,0,1:T(1,128)}), s32[1,16,8]{2,0,1:T(1,128)S(1)}, u32[]{:S(2)}, u32[]{:S(2)}) async-start(s32[1,16,8]{2,0,1:T(1,128)} %copy.33), calls=%async_computation | async-start | bytes 16384 | tf_op jit(solution)/shard_map/all_to_all | solution.py:110
  74.8 13.2 %copy-start.1 = (bf16[128,512]{1,0:T(8,128)(2,1)S(1)}, bf16[128,512]{1,0:T(8,128)(2,1)}, u32[]{:S(2)}) copy-start(bf16[128,512]{1,0:T(8,128)(2,1)} %add_convert_fusion.3) | copy-start | bytes 393220
  88.0 9.3 %copy-start.3 = (bf16[512,512]{1,0:T(8,128)(2,1)S(1)}, bf16[512,512]{1,0:T(8,128)(2,1)}, u32[]{:S(2)}) copy-start(bf16[512,512]{1,0:T(8,128)(2,1)} %param.56) | copy-start | bytes 1572868
  97.5 17.1 %copy-start.2 = (bf16[512,512]{1,0:T(8,128)(2,1)S(1)}, bf16[512,512]{1,0:T(8,128)(2,1)}, u32[]{:S(2)}) copy-start(bf16[512,512]{1,0:T(8,128)(2,1)} %param.51) | copy-start | bytes 1572868
  114.6 4.8 %copy-start.19 = (f32[512]{0:T(512)S(1)}, f32[512]{0:T(512)}, u32[]{:S(2)}) copy-start(f32[512]{0:T(512)} %param.55) | copy-start | bytes 6148
  114.6 4.8 %copy-start.20 = (f32[512]{0:T(512)S(1)}, f32[512]{0:T(512)}, u32[]{:S(2)}) copy-start(f32[512]{0:T(512)} %param.53) | copy-start | bytes 6148
  119.5 7.2 %copy-start.21 = (f32[512]{0:T(512)S(1)}, f32[512]{0:T(512)}, u32[]{:S(2)}) copy-start(f32[512]{0:T(512)} %param.58) | copy-start | bytes 6148
  119.5 9.6 %copy-start.4 = (bf16[512,512]{1,0:T(8,128)(2,1)S(1)}, bf16[512,512]{1,0:T(8,128)(2,1)}, u32[]{:S(2)}) copy-start(bf16[512,512]{1,0:T(8,128)(2,1)} %param.59) | copy-start | bytes 1572868
  119.5 9.6 %copy-start.11 = (f32[512]{0:T(512)S(1)}, f32[512]{0:T(512)}, u32[]{:S(2)}) copy-start(f32[512]{0:T(512)} %param.60) | copy-start | bytes 6148
  126.7 2.9 %copy-start.12 = (f32[512]{0:T(512)S(1)}, f32[512]{0:T(512)}, u32[]{:S(2)}) copy-start(f32[512]{0:T(512)} %param.61) | copy-start | bytes 6148
Sparse Core Ops, SparseCore 0:
  57.7 45.7 all-gather.1
where the time goes:
time: 138 us; the launch traced here: 137 us
  local copies, waits for them, and re-layouts  53.1 us (38%)
  matrix products  39.2 us (28%)
  waiting for transfers between devices  14.9 us (11%)
  between operations  13.8 us (10%)
  starting transfers between devices  12.7 us (9%)
  other arithmetic  3.52 us (3%)
    gather x2, local copies, waits for them, and re-layouts, shards(): sender_latent = everything[lookup[mesh_senders]]  24.2 us
    gather x1, local copies, waits for them, and re-layouts, shards(): grid_lat[enc_src]  17.3 us
    gather x1, local copies, waits for them, and re-layouts, shards(): mesh_mid[mesh_recv]  9.24 us
    all_to_all x1, starting transfers between devices, shards(): lax.all_to_all(mesh_send, 'lat', split_axis=1, concat_axis=0, tiled=True)  9.02 us
    dot_general x1, matrix products, shards(): jnp.dot(hidden, w_enc_out, preferred_element_type=jnp.float32) + b_enc_out  8.02 us
    dot_general x1, matrix products, shards(): jnp.dot(grid_lat[enc_src], w_enc_grid, preferred_element_type=jnp.float32)  7.93 us
    dot_general x1, matrix products, shards(): jnp.dot(hidden, w_edge_out, preferred_element_type=jnp.float32) + b_edge_out  7.18 us
    all_to_all x1, waiting for transfers between devices, shards(): lax.all_to_all(mesh_send, 'lat', split_axis=1, concat_axis=0, tiled=True)  6.15 us
  transfers between devices with their start and end apart: 4, of which 3 were waited for; matrix products, arithmetic and copies ran while one was open for 19% of the time, Pallas kernels for 0%

commit v1 on v0

v1 whole, which is shorter than its diff:
```python
import functools

import jax
import jax.numpy as jnp
from jax import lax
from jax.experimental import pallas as pl
from jax.experimental.pallas import tpu as pltpu
from jax.sharding import PartitionSpec as P

F32 = jnp.float32
BF16 = jnp.bfloat16
LANES = 128
MESH_ID = pl.DeviceIdType.MESH
VMEM_BYTES = 48 * 1024 * 1024


def silu(x):
    half = 0.5 * x
    return half + half * jnp.tanh(half)


def dot(a, b):
    return jnp.dot(a, b, preferred_element_type=F32)


def dot_nt(a, b):
    return lax.dot_general(a, b, (((1,), (1,)), ((), ())), preferred_element_type=F32)


def dot_tn(a, b):
    return lax.dot_general(a, b, (((0,), (0,)), ((), ())), preferred_element_type=F32)


def split_dot(a, w):
    high = a.astype(BF16)
    low = (a - high.astype(F32)).astype(BF16)
    return dot(high, w) + dot(low, w)


def layer_norm(values, gain):
    center = values - jnp.mean(values, -1, keepdims=True)
    spread = jnp.mean(center * center, -1, keepdims=True)
    return center * lax.rsqrt(spread + 1e-05) * gain


def encode_kernel(
    src, grid_lat, feat, dst, w_grid, w_feat, b_enc, w_out, b_out, out, table, even, odd, acc, cnt
):
    grid_rows, width = grid_lat.shape
    edges = dst.shape[1]
    keys = out.shape[0]
    parts = width // LANES
    block = even.shape[0] // parts
    blocks = edges // block
    rows = 256

    def project(i, carry):
        p = dot(grid_lat[pl.ds(pl.multiple_of(i * rows, rows), rows), :], w_grid[...]) + b_enc[...]
        for j in range(parts):
            table[pl.ds(i * (rows * parts) + j, rows, stride=parts), :] = p[
                :, j * LANES : (j + 1) * LANES
            ]
        return carry

    lax.fori_loop(0, grid_rows // rows, project, 0)
    acc[...] = jnp.zeros_like(acc)
    cnt[...] = jnp.zeros_like(cnt)

    def gather(turn, held):
        base = turn * block
        for r in range(block):
            row = pl.multiple_of(src[base + r] * parts, parts)
            held[pl.ds(r * parts, parts), :] = table[pl.ds(row, parts), :]

    def compute(turn, held):
        cols = pl.ds(pl.multiple_of(turn * block, block), block)
        from_feat = dot_tn(feat[:, cols], w_feat[...])
        pieces = []
        for j in range(parts):
            x = held[pl.ds(j, block, stride=parts), :] + from_feat[:, j * LANES : (j + 1) * LANES]
            pieces.append(silu(x).astype(BF16))
        hidden = jnp.concatenate(pieces, axis=1)
        labels = lax.broadcasted_iota(jnp.int32, (keys, block), 0)
        hit = jnp.where(dst[:, cols] == labels, 1.0, 0.0).astype(F32)
        acc[...] += dot(hit.astype(BF16), hidden)
        total = hit[:, :LANES]
        for j in range(1, block // LANES):
            total = total + hit[:, j * LANES : (j + 1) * LANES]
        cnt[...] += total

    gather(0, even)

    def pair(k, carry):
        gather(2 * k + 1, odd)
        compute(2 * k, even)
        gather(jnp.minimum(2 * k + 2, blocks - 1), even)
        compute(2 * k + 1, odd)
        return carry

    lax.fori_loop(0, blocks // 2, pair, 0)
    count = jnp.sum(cnt[...], axis=1, keepdims=True)
    out[...] = (split_dot(acc[...], w_out[...]) + count * b_out[...]).astype(BF16)


def encode(grid_lat, feat, src, dst, w_grid, w_feat, b_enc, w_out, b_out, keys):
    width = grid_lat.shape[1]
    parts = width // LANES
    block = 256
    vmem = pl.BlockSpec(memory_space=pltpu.VMEM)
    edges = src.shape[0]
    return pl.pallas_call(
        encode_kernel,
        name="encode",
        out_shape=jax.ShapeDtypeStruct((keys, width), BF16),
        in_specs=[pl.BlockSpec(memory_space=pltpu.SMEM)] + [vmem] * 8,
        out_specs=vmem,
        scratch_shapes=[
            pltpu.VMEM((grid_lat.shape[0] * parts, LANES), F32),
            pltpu.VMEM((block * parts, LANES), F32),
            pltpu.VMEM((block * parts, LANES), F32),
            pltpu.VMEM((keys, width), F32),
            pltpu.VMEM((keys, LANES), F32),
        ],
        compiler_params=pltpu.CompilerParams(vmem_limit_bytes=VMEM_BYTES),
        cost_estimate=pl.CostEstimate(
            flops=2 * width * (grid_lat.shape[0] * width + edges * keys),
            bytes_accessed=2 * width * (grid_lat.shape[0] + 2 * width),
            transcendentals=edges * width,
        ),
    )(src, grid_lat, feat, dst, w_grid, w_feat, b_enc, w_out, b_out)


def process_kernel(
    peers,
    part,
    mesh_lat,
    mesh_send,
    senders,
    receivers,
    w_node_self_h,
    w_node_agg_h,
    w_node_out_h,
    w_edge_send_h,
    w_edge_recv_h,
    w_edge_out_h,
    w_proc_self_h,
    w_proc_agg_h,
    w_proc_out_h,
    b_node,
    b_node_out,
    gain_node,
    b_edge,
    b_edge_out,
    b_proc,
    b_proc_out,
    gain_proc,
    out,
    weights,
    below,
    above,
    outbox,
    inbox,
    chosen,
    hits_send,
    hits_recv,
    preact,
    weight_sem,
    halo_send_sem,
    halo_recv_sem,
    rows_send_sem,
    rows_recv_sem,
    own_sem,
):
    me = lax.axis_index("lat")
    patch, width = mesh_lat.shape
    half = width // 2
    cap = mesh_send.shape[2]
    two = 2 * cap
    edges = senders.shape[1]
    slots = peers * cap
    column = min(edges, 512)

    sources = (
        w_node_self_h,
        w_node_agg_h,
        w_node_out_h,
        w_edge_recv_h,
        w_edge_send_h,
        w_proc_self_h,
        w_edge_out_h,
        w_proc_agg_h,
        w_proc_out_h,
    )
    loads = [
        pltpu.make_async_copy(ref, weights.at[n], weight_sem.at[n]) for n, ref in enumerate(sources)
    ]
    for load in loads:
        load.start()

    barrier = pltpu.get_barrier_semaphore()

    def greet(k, carry):
        peer = lax.rem(me + k, peers)
        pl.semaphore_signal(barrier, inc=1, device_id={"lat": peer}, device_id_type=MESH_ID)
        return carry

    lax.fori_loop(1, peers, greet, 0)

    loads[0].wait()
    latent = mesh_lat[...]
    self_term = dot(latent, weights[0]) + b_node[...]

    pl.semaphore_wait(barrier, peers - 1)

    to_low = pltpu.make_async_remote_copy(
        src_ref=part.at[pl.ds(0, patch)],
        dst_ref=above,
        send_sem=halo_send_sem.at[0],
        recv_sem=halo_recv_sem.at[0],
        device_id={"lat": jnp.maximum(me - 1, 0)},
        device_id_type=MESH_ID,
    )
    to_high = pltpu.make_async_remote_copy(
        src_ref=part.at[pl.ds(2 * patch, patch)],
        dst_ref=below,
        send_sem=halo_send_sem.at[1],
        recv_sem=halo_recv_sem.at[1],
        device_id={"lat": jnp.minimum(me + 1, peers - 1)},
        device_id_type=MESH_ID,
    )

    @pl.when(me > 0)
    def _():
        to_low.start()

    @pl.when(me < peers - 1)
    def _():
        to_high.start()

    @pl.when(me == 0)
    def _():
        below[...] = jnp.zeros_like(below)

    @pl.when(me == peers - 1)
    def _():
        above[...] = jnp.zeros_like(above)

    picks = mesh_send[0].astype(F32)[:, None, :]
    row = lax.broadcasted_iota(jnp.int32, (peers, two, cap), 1)
    lane = lax.broadcasted_iota(jnp.int32, (peers, two, cap), 2)
    spread = jnp.where(lax.rem(row, cap) == lane, jnp.broadcast_to(picks, row.shape), 0.0)
    pick = jnp.sum(spread, axis=2, keepdims=True)
    side = lax.broadcasted_iota(jnp.int32, (peers, two, 1), 1) // cap
    pick = pick + (side * patch).astype(F32)
    spot = lax.broadcasted_iota(jnp.int32, (peers, two, 2 * patch), 2).astype(F32)
    chosen[...] = (
        jnp.where(spot == pick, 1.0, 0.0).reshape(peers * two, 2 * patch).astype(BF16)
    )

    labels = lax.broadcasted_iota(jnp.int32, (patch, edges), 0)
    hit = jnp.where(receivers[...] == labels, 1.0, 0.0).astype(F32)
    hits_recv[...] = hit.astype(BF16)
    count = jnp.sum(hit, axis=1, keepdims=True)
    for n in range((patch + slots) // patch):
        hits_send[n * patch : (n + 1) * patch, :] = jnp.where(
            senders[...] == labels + n * patch, 1.0, 0.0
        ).astype(BF16)

    @pl.when(me < peers - 1)
    def _():
        to_low.wait_recv()

    @pl.when(me > 0)
    def _():
        to_high.wait_recv()

    summed = (
        part[pl.ds(patch, patch), :].astype(F32) + above[...].astype(F32) + below[...].astype(F32)
    ).astype(BF16)
    loads[1].wait()
    hidden = silu(self_term + dot(summed, weights[1])).astype(BF16)
    loads[2].wait()
    update = dot(hidden, weights[2]) + b_node_out[...]
    mid = (latent.astype(F32) + layer_norm(update, gain_node[...])).astype(BF16)

    halves = jnp.concatenate([mid[:, :half], mid[:, half:]], axis=0)
    outbox[...] = dot(chosen[...], halves).astype(BF16)

    def send(k, carry):
        peer = lax.rem(me + k, peers)
        pltpu.make_async_remote_copy(
            src_ref=outbox.at[pl.ds(pl.multiple_of(peer * two, two), two)],
            dst_ref=inbox.at[pl.ds(pl.multiple_of(me * two, two), two)],
            send_sem=rows_send_sem,
            recv_sem=rows_recv_sem,
            device_id={"lat": peer},
            device_id_type=MESH_ID,
        ).start()
        return carry

    lax.fori_loop(1, peers, send, 0)
    mine = pl.ds(pl.multiple_of(me * two, two), two)
    own = pltpu.make_async_copy(outbox.at[mine], inbox.at[mine], own_sem)
    own.start()

    loads[3].wait()
    loads[4].wait()
    recv_table = (dot(mid, weights[3]) + b_edge[...]).T.astype(BF16)
    near_table = dot(mid, weights[4]).T.astype(BF16)
    local_table = jnp.concatenate([recv_table, near_table], axis=1)
    for n in range(edges // column):
        cols = slice(n * column, (n + 1) * column)
        preact[:, cols] = dot(
            local_table,
            jnp.concatenate([hits_recv[:, cols], hits_send[:patch, cols]], axis=0),
        )
    loads[5].wait()
    proc_term = dot(mid, weights[5]) + b_proc[...]

    own.wait()
    others = pl.ds(0, (peers - 1) * two)
    pltpu.make_async_copy(inbox.at[others], inbox.at[others], rows_recv_sem).wait()

    top = dot(inbox[...], weights[4, :half, :]).reshape(peers, two, width)
    low = dot(inbox[...], weights[4, half:, :]).reshape(peers, two, width)
    far_table = (top[:, :cap, :] + low[:, cap:, :]).reshape(slots, width).T.astype(BF16)
    gathered = jnp.zeros((patch, width), F32)
    for n in range(edges // column):
        cols = slice(n * column, (n + 1) * column)
        x = preact[:, cols] + dot(far_table, hits_send[patch:, cols])
        gathered = gathered + dot_nt(hits_recv[:, cols], silu(x).astype(BF16))
    loads[6].wait()
    summed = (split_dot(gathered, weights[6]) + count * b_edge_out[...]).astype(BF16)
    loads[7].wait()
    hidden = silu(proc_term + dot(summed, weights[7])).astype(BF16)
    loads[8].wait()
    update = dot(hidden, weights[8]) + b_proc_out[...]
    out[...] = (mid.astype(F32) + layer_norm(update, gain_proc[...])).astype(BF16)

    @pl.when(me > 0)
    def _():
        to_low.wait_send()

    @pl.when(me < peers - 1)
    def _():
        to_high.wait_send()

    pltpu.make_async_copy(outbox.at[others], outbox.at[others], rows_send_sem).wait()


def process(peers, part, mesh_lat, mesh_send, senders, receivers, mats, vectors):
    patch, width = mesh_lat.shape
    cap = mesh_send.shape[2]
    edges = senders.shape[1]
    slots = peers * cap
    vmem = pl.BlockSpec(memory_space=pltpu.VMEM)
    hbm = pl.BlockSpec(memory_space=pl.ANY)
    return pl.pallas_call(
        functools.partial(process_kernel, peers),
        name="process",
        out_shape=jax.ShapeDtypeStruct((patch, width), BF16),
        in_specs=[vmem] * 5 + [hbm] * len(mats) + [vmem] * len(vectors),
        out_specs=vmem,
        scratch_shapes=[
            pltpu.VMEM((len(mats), width, width), BF16),
            pltpu.VMEM((patch, width), BF16),
            pltpu.VMEM((patch, width), BF16),
            pltpu.VMEM((2 * slots, width // 2), BF16),
            pltpu.VMEM((2 * slots, width // 2), BF16),
            pltpu.VMEM((2 * slots, 2 * patch), BF16),
            pltpu.VMEM((patch + slots, edges), BF16),
            pltpu.VMEM((patch, edges), BF16),
            pltpu.VMEM((width, edges), F32),
            pltpu.SemaphoreType.DMA((len(mats),)),
            pltpu.SemaphoreType.DMA((2,)),
            pltpu.SemaphoreType.DMA((2,)),
            pltpu.SemaphoreType.DMA,
            pltpu.SemaphoreType.DMA,
            pltpu.SemaphoreType.DMA,
        ],
        compiler_params=pltpu.CompilerParams(
            collective_id=0, has_side_effects=True, vmem_limit_bytes=VMEM_BYTES
        ),
    )(part, mesh_lat, mesh_send, senders, receivers, *mats, *vectors)


def shards(
    grid_lat,
    mesh_lat,
    enc_feat,
    enc_src,
    enc_dst,
    mesh_send,
    mesh_senders,
    mesh_recv,
    w_enc_grid,
    w_enc_feat,
    b_enc,
    w_enc_out,
    b_enc_out,
    w_node_self,
    w_node_agg,
    b_node,
    w_node_out,
    b_node_out,
    gain_node,
    w_edge_send,
    w_edge_recv,
    b_edge,
    w_edge_out,
    b_edge_out,
    w_proc_self,
    w_proc_agg,
    b_proc,
    w_proc_out,
    b_proc_out,
    gain_proc,
):
    peers = lax.axis_size("lat")
    patch = mesh_lat.shape[0]

    def line(v):
        return v.reshape(1, -1)

    part = encode(
        grid_lat,
        enc_feat,
        enc_src,
        line(enc_dst),
        w_enc_grid,
        w_enc_feat,
        line(b_enc),
        w_enc_out,
        line(b_enc_out),
        3 * patch,
    )
    return process(
        peers,
        part,
        mesh_lat,
        mesh_send,
        line(mesh_senders),
        line(mesh_recv),
        (
            w_node_self,
            w_node_agg,
            w_node_out,
            w_edge_send,
            w_edge_recv,
            w_edge_out,
            w_proc_self,
            w_proc_agg,
            w_proc_out,
        ),
        tuple(
            line(v)
            for v in (
                b_node,
                b_node_out,
                gain_node,
                b_edge,
                b_edge_out,
                b_proc,
                b_proc_out,
                gain_proc,
            )
        ),
    )


def solution(mesh):
    rows = P(("groups", "lat"), None)
    flat = P(("groups", "lat"))
    placed = (
        rows,
        rows,
        P(None, ("groups", "lat")),
        flat,
        flat,
        P(("groups", "lat"), None, None),
        flat,
        flat,
    ) + (P(),) * 22
    return jax.shard_map(
        shards, mesh=mesh, in_specs=placed, out_specs=P(("groups", "lat"), None), check_vma=False
    )
```

time: 138 us -> 42 us (0.30)
  local copies, waits for them, and re-layouts: 53.1 us -> 9.44 us
  matrix products: 39.2 us -> 0 us
  Pallas kernels: 0 us -> 31.7 us
  waiting for transfers between devices: 14.9 us -> 0 us
  between operations: 13.8 us -> 0.31 us
  starting transfers between devices: 12.7 us -> 0 us
  other arithmetic: 3.52 us -> 0 us
    gather x4 -> x0, local copies, waits for them, and re-layouts: 50.8 us -> none  [the longest x2 24.2 us: shards(): sender_latent = everything[lookup[mesh_senders]]]
    dot_general x11 -> x0, matrix products: 39.2 us -> none  [the longest x1 8.02 us: shards(): jnp.dot(hidden, w_enc_out, preferred_element_type=jnp.float32) + b_enc_out]
    pallas_call x0 -> x2, Pallas kernels: none -> 31.7 us  [the longest x1 18.5 us: process(): pl.pallas_call(functools.partial(process_kernel, peers), name='process',...]
    all_to_all x1 -> x0, starting transfers between devices: 9.02 us -> none  [shards(): lax.all_to_all(mesh_send, 'lat', split_axis=1, concat_axis=0, tiled=True)]
    unnamed x45 -> x60, local copies, waits for them, and re-layouts: 1.49 us -> 9.44 us
    all_to_all x1 -> x0, waiting for transfers between devices: 6.15 us -> none  [shards(): lax.all_to_all(mesh_send, 'lat', split_axis=1, concat_axis=0, tiled=True)]
    all_gather x1 -> x0, waiting for transfers between devices: 5.96 us -> none  [shards(): everything = lax.all_gather(mesh_mid, 'lat', axis=0, tiled=True)]
    ppermute x2 -> x0, starting transfers between devices: 3.66 us -> none  [the longest x1 2.37 us: extended(): lax.ppermute(lax.slice_in_dim(block, block.shape[dim] - width, None, axis...]
  transfers between devices with their start and end apart: 4 -> 0, of which waited for: 3 -> 0; matrix products, arithmetic and copies ran while one was open for 19% -> 0% of each run, Pallas kernels for 0% -> 0%
where the time goes in v1:
time: 42 us; the launch traced here: 41.4 us
  Pallas kernels  31.7 us (75%)
  local copies, waits for them, and re-layouts  9.44 us (22%)
    pallas_call x1, Pallas kernels, process(): pl.pallas_call(functools.partial(process_kernel, peers), name='process',...  18.5 us
    pallas_call x1, Pallas kernels, encode(): pl.pallas_call(encode_kernel, name='encode', out_shape=jax.ShapeDtypeStru...  13.2 us
    unnamed x60, local copies, waits for them, and re-layouts  9.44 us

profile of v1, /device:TPU:0, one launch (start us, length us, event | category | flops | bytes accessed | tf_op | source)
XLA Modules:
  0.0 41.4 jit_solution(11032560509154658122)
XLA Ops:
  0.0 0.8 %copy.31.mesh_send = s32[1,16,8]{2,1,0:T(8,128)S(1)} copy(s32[1,16,8]{1,2,0:T(8,128)} %param.35) | data formatting | bytes 1024 | tf_op args[5]
  0.8 0.0 copy-start.20
  0.8 1.6 %copy-done.20 = bf16[2048,512]{1,0:T(8,128)(2,1)S(1)} copy-done((bf16[2048,512]{1,0:T(8,128)(2,1)S(1)}, bf16[2048,512]{1,0:T(8,128)(2,1)}, u32[]{:S(2)}) %copy-start.20) | copy-done | bytes 2097176
  2.3 0.0 copy-start.21
  2.4 1.0 %copy-done.21 = bf16[512,512]{1,0:T(8,128)(2,1)S(1)} copy-done((bf16[512,512]{1,0:T(8,128)(2,1)S(1)}, bf16[512,512]{1,0:T(8,128)(2,1)}, u32[]{:S(2)}) %copy-start.21) | copy-done | bytes 524312
  3.4 0.0 copy-start.22
  3.4 1.0 %copy-done.22 = bf16[512,512]{1,0:T(8,128)(2,1)S(1)} copy-done((bf16[512,512]{1,0:T(8,128)(2,1)S(1)}, bf16[512,512]{1,0:T(8,128)(2,1)}, u32[]{:S(2)}) %copy-start.22) | copy-done | bytes 524312
  4.4 0.0 copy-start.23
  4.4 0.8 %copy-done.23 = bf16[4,4096]{1,0:T(4,128)(2,1)S(1)} copy-done((bf16[4,4096]{1,0:T(4,128)(2,1)S(1)}, bf16[4,4096]{1,0:T(4,128)(2,1)}, u32[]{:S(2)}) %copy-start.23) | copy-done | bytes 32792
  5.2 0.0 copy-start.24
  5.2 0.7 %copy-done.24 = s32[4096]{0:T(1024)S(1)} copy-done((s32[4096]{0:T(1024)S(1)}, s32[4096]{0:T(1024)}, u32[]{:S(2)}) %copy-start.24) | copy-done | bytes 16408
  5.9 0.0 copy-start.25
  5.9 0.7 %copy-done.25 = s32[4096]{0:T(1024)S(1)} copy-done((s32[4096]{0:T(1024)S(1)}, s32[4096]{0:T(1024)}, u32[]{:S(2)}) %copy-start.25) | copy-done | bytes 16408
  6.6 0.0 copy-start.26
  6.6 0.7 %copy-done.26 = bf16[4,512]{1,0:T(4,128)(2,1)S(1)} copy-done((bf16[4,512]{1,0:T(4,128)(2,1)S(1)}, bf16[4,512]{1,0:T(4,128)(2,1)}, u32[]{:S(2)}) %copy-start.26) | copy-done | bytes 4120
  7.3 0.0 copy-start.27
  7.3 0.7 %copy-done.27 = f32[512]{0:T(512)S(1)} copy-done((f32[512]{0:T(512)S(1)}, f32[512]{0:T(512)}, u32[]{:S(2)}) %copy-start.27) | copy-done | bytes 2072
  8.0 0.0 copy-start.28
  8.0 0.7 %copy-done.28 = f32[512]{0:T(512)S(1)} copy-done((f32[512]{0:T(512)S(1)}, f32[512]{0:T(512)}, u32[]{:S(2)}) %copy-start.28) | copy-done | bytes 2072
  8.7 0.0 copy-start
  8.7 0.0 copy-start.1
  8.7 0.0 copy-start.2
  8.7 0.0 copy-start.3
  8.7 0.0 copy-start.4
  8.7 0.0 copy-start.5
  8.7 0.0 copy-start.6
  8.7 0.0 copy-start.7
  8.7 0.0 copy-start.8
  8.8 0.0 copy-start.9
  8.8 0.0 copy-start.10
  8.8 0.0 copy-start.11
  8.8 0.0 copy-start.12
  8.8 0.0 copy-start.13
  8.8 0.0 copy-start.14
  8.8 0.0 copy-start.15
  8.8 0.0 copy-start.16
  8.8 0.0 copy-start.17
  8.9 0.0 copy-start.18
  8.9 0.0 copy-start.19
  8.9 13.2 %encode.1.part = bf16[384,512]{1,0:T(8,128)(2,1)S(1)} custom-call(s32[4096]{0:T(1024)S(1)} %copy-done.24, bf16[2048,512]{1,0:T(8,128)(2,1)S(1)} %copy-done.20, bf16[4,4096]{1,0:T(4,128)(2,1)S(1)} %copy-done.23, s32[1,4096]{1,0:T(1,128)S(1)} %bitcast.23, bf16[512,512]{1,0:T(8,128)(2,1)S(1)} %copy-done.21, bf16[4,512]{1,0:T(4,128)(2,1)S(1)} %copy-done.26, ...), custom_call_target="tpu_custom_call" | custom-call | flops 2684354560 | bytes 3145728 | tf_op jit(solution)/shard_map/encode/pallas_call | solution.py:111
  22.1 0.0 copy-done
  22.1 0.0 copy-done.1
  22.1 0.0 copy-done.2
  22.1 0.0 copy-done.3
  22.1 0.0 copy-done.4
  22.1 0.0 copy-done.5
  22.1 0.0 copy-done.6
  22.2 0.0 copy-done.7
  22.2 0.0 copy-done.8
  22.2 0.0 copy-done.9
  22.2 0.0 copy-done.10
  22.2 0.0 copy-done.11
  22.2 0.0 copy-done.12
  22.2 0.0 copy-done.13
  22.2 0.0 copy-done.14
  22.2 0.0 copy-done.15
  22.2 0.0 copy-done.16
  22.3 0.0 copy-done.17
  22.3 0.0 copy-done.18
  22.3 0.0 copy-done.19
  22.3 18.5 %process.1 = bf16[128,512]{1,0:T(8,128)(2,1)S(1)} custom-call(bf16[384,512]{1,0:T(8,128)(2,1)S(1)} %encode.1.part, bf16[128,512]{1,0:T(8,128)(2,1)S(1)} %copy-done.9, s32[1,16,8]{2,1,0:T(8,128)S(1)} %copy.31.mesh_send, s32[1,2048]{1,0:T(1,128)S(1)} %bitcast.13, s32[1,2048]{1,0:T(1,128)S(1)} %bitcast.14, bf16[512,512]{1,0:T(8,128)(2,1)S(1)} %copy-done, ...), custom_call_target="tpu_custom_call" | custom-call | tf_op jit(solution)/shard_map/process/pallas_call | solution.py:358
  40.8 0.7 %copy.33 = bf16[128,512]{1,0:T(8,128)(2,1)} copy(bf16[128,512]{1,0:T(8,128)(2,1)S(1)} %process.1) | data formatting | bytes 262144
Async XLA Ops:
  0.8 1.6 %copy-start.20 = (bf16[2048,512]{1,0:T(8,128)(2,1)S(1)}, bf16[2048,512]{1,0:T(8,128)(2,1)}, u32[]{:S(2)}) copy-start(bf16[2048,512]{1,0:T(8,128)(2,1)} %grid_lat.1) | copy-start | bytes 6291460
  2.3 1.0 %copy-start.21 = (bf16[512,512]{1,0:T(8,128)(2,1)S(1)}, bf16[512,512]{1,0:T(8,128)(2,1)}, u32[]{:S(2)}) copy-start(bf16[512,512]{1,0:T(8,128)(2,1)} %w_grid.1) | copy-start | bytes 1572868
  3.4 1.0 %copy-start.22 = (bf16[512,512]{1,0:T(8,128)(2,1)S(1)}, bf16[512,512]{1,0:T(8,128)(2,1)}, u32[]{:S(2)}) copy-start(bf16[512,512]{1,0:T(8,128)(2,1)} %w_out.1) | copy-start | bytes 1572868
  4.4 0.8 %copy-start.23 = (bf16[4,4096]{1,0:T(4,128)(2,1)S(1)}, bf16[4,4096]{1,0:T(4,128)(2,1)}, u32[]{:S(2)}) copy-start(bf16[4,4096]{1,0:T(4,128)(2,1)} %feat.1) | copy-start | bytes 98308
  5.2 0.7 %copy-start.24 = (s32[4096]{0:T(1024)S(1)}, s32[4096]{0:T(1024)}, u32[]{:S(2)}) copy-start(s32[4096]{0:T(1024)} %src.1) | copy-start | bytes 49156
  5.9 0.7 %copy-start.25 = (s32[4096]{0:T(1024)S(1)}, s32[4096]{0:T(1024)}, u32[]{:S(2)}) copy-start(s32[4096]{0:T(1024)} %param.34) | copy-start | bytes 49156
  6.6 0.7 %copy-start.26 = (bf16[4,512]{1,0:T(4,128)(2,1)S(1)}, bf16[4,512]{1,0:T(4,128)(2,1)}, u32[]{:S(2)}) copy-start(bf16[4,512]{1,0:T(4,128)(2,1)} %w_feat.1) | copy-start | bytes 12292
  7.3 0.7 %copy-start.27 = (f32[512]{0:T(512)S(1)}, f32[512]{0:T(512)}, u32[]{:S(2)}) copy-start(f32[512]{0:T(512)} %param.40) | copy-start | bytes 6148
  8.0 0.7 %copy-start.28 = (f32[512]{0:T(512)S(1)}, f32[512]{0:T(512)}, u32[]{:S(2)}) copy-start(f32[512]{0:T(512)} %param.42) | copy-start | bytes 6148
  8.7 13.4 %copy-start = (bf16[512,512]{1,0:T(8,128)(2,1)S(1)}, bf16[512,512]{1,0:T(8,128)(2,1)}, u32[]{:S(2)}) copy-start(bf16[512,512]{1,0:T(8,128)(2,1)} %w_node_self_h.1) | copy-start | bytes 1572868
  8.7 13.4 %copy-start.1 = (bf16[512,512]{1,0:T(8,128)(2,1)S(1)}, bf16[512,512]{1,0:T(8,128)(2,1)}, u32[]{:S(2)}) copy-start(bf16[512,512]{1,0:T(8,128)(2,1)} %w_node_agg_h.1) | copy-start | bytes 1572868
  8.7 13.4 %copy-start.2 = (bf16[512,512]{1,0:T(8,128)(2,1)S(1)}, bf16[512,512]{1,0:T(8,128)(2,1)}, u32[]{:S(2)}) copy-start(bf16[512,512]{1,0:T(8,128)(2,1)} %w_node_out_h.1) | copy-start | bytes 1572868
  8.7 13.4 %copy-start.3 = (bf16[512,512]{1,0:T(8,128)(2,1)S(1)}, bf16[512,512]{1,0:T(8,128)(2,1)}, u32[]{:S(2)}) copy-start(bf16[512,512]{1,0:T(8,128)(2,1)} %w_edge_send_h.1) | copy-start | bytes 1572868
  8.7 13.4 %copy-start.4 = (bf16[512,512]{1,0:T(8,128)(2,1)S(1)}, bf16[512,512]{1,0:T(8,128)(2,1)}, u32[]{:S(2)}) copy-start(bf16[512,512]{1,0:T(8,128)(2,1)} %w_edge_recv_h.1) | copy-start | bytes 1572868
  8.7 13.4 %copy-start.5 = (bf16[512,512]{1,0:T(8,128)(2,1)S(1)}, bf16[512,512]{1,0:T(8,128)(2,1)}, u32[]{:S(2)}) copy-start(bf16[512,512]{1,0:T(8,128)(2,1)} %w_edge_out_h.1) | copy-start | bytes 1572868
  8.7 13.4 %copy-start.6 = (bf16[512,512]{1,0:T(8,128)(2,1)S(1)}, bf16[512,512]{1,0:T(8,128)(2,1)}, u32[]{:S(2)}) copy-start(bf16[512,512]{1,0:T(8,128)(2,1)} %w_proc_self_h.1) | copy-start | bytes 1572868
  8.7 13.4 %copy-start.7 = (bf16[512,512]{1,0:T(8,128)(2,1)S(1)}, bf16[512,512]{1,0:T(8,128)(2,1)}, u32[]{:S(2)}) copy-start(bf16[512,512]{1,0:T(8,128)(2,1)} %w_proc_agg_h.1) | copy-start | bytes 1572868
  8.7 13.4 %copy-start.8 = (bf16[512,512]{1,0:T(8,128)(2,1)S(1)}, bf16[512,512]{1,0:T(8,128)(2,1)}, u32[]{:S(2)}) copy-start(bf16[512,512]{1,0:T(8,128)(2,1)} %w_proc_out_h.1) | copy-start | bytes 1572868
  8.8 13.4 %copy-start.9 = (bf16[128,512]{1,0:T(8,128)(2,1)S(1)}, bf16[128,512]{1,0:T(8,128)(2,1)}, u32[]{:S(2)}) copy-start(bf16[128,512]{1,0:T(8,128)(2,1)} %mesh_lat.1) | copy-start | bytes 393220
  8.8 13.4 %copy-start.10 = (s32[2048]{0:T(1024)S(1)}, s32[2048]{0:T(1024)}, u32[]{:S(2)}) copy-start(s32[2048]{0:T(1024)} %param.36) | copy-start | bytes 24580
  8.8 13.4 %copy-start.11 = (s32[2048]{0:T(1024)S(1)}, s32[2048]{0:T(1024)}, u32[]{:S(2)}) copy-start(s32[2048]{0:T(1024)} %param.37) | copy-start | bytes 24580
  8.8 13.4 %copy-start.12 = (f32[512]{0:T(512)S(1)}, f32[512]{0:T(512)}, u32[]{:S(2)}) copy-start(f32[512]{0:T(512)} %param.45) | copy-start | bytes 6148
  8.8 13.4 %copy-start.13 = (f32[512]{0:T(512)S(1)}, f32[512]{0:T(512)}, u32[]{:S(2)}) copy-start(f32[512]{0:T(512)} %param.47) | copy-start | bytes 6148
  8.8 13.4 %copy-start.14 = (f32[512]{0:T(512)S(1)}, f32[512]{0:T(512)}, u32[]{:S(2)}) copy-start(f32[512]{0:T(512)} %param.48) | copy-start | bytes 6148
  8.8 13.4 %copy-start.15 = (f32[512]{0:T(512)S(1)}, f32[512]{0:T(512)}, u32[]{:S(2)}) copy-start(f32[512]{0:T(512)} %param.51) | copy-start | bytes 6148
  8.8 13.4 %copy-start.16 = (f32[512]{0:T(512)S(1)}, f32[512]{0:T(512)}, u32[]{:S(2)}) copy-start(f32[512]{0:T(512)} %param.53) | copy-start | bytes 6148
  8.8 13.4 %copy-start.17 = (f32[512]{0:T(512)S(1)}, f32[512]{0:T(512)}, u32[]{:S(2)}) copy-start(f32[512]{0:T(512)} %param.56) | copy-start | bytes 6148
  8.9 13.4 %copy-start.18 = (f32[512]{0:T(512)S(1)}, f32[512]{0:T(512)}, u32[]{:S(2)}) copy-start(f32[512]{0:T(512)} %param.58) | copy-start | bytes 6148
  8.9 13.4 %copy-start.19 = (f32[512]{0:T(512)S(1)}, f32[512]{0:T(512)}, u32[]{:S(2)}) copy-start(f32[512]{0:T(512)} %param.59) | copy-start | bytes 6148

commit v2 on v1

--- a/solution.py
+++ b/solution.py
@@ -11,7 +11,9 @@
 BF16 = jnp.bfloat16
 LANES = 128
 MESH_ID = pl.DeviceIdType.MESH
-VMEM_BYTES = 48 * 1024 * 1024
+VMEM_BYTES = 63 * 1024 * 1024 + 512 * 1024
+PIECES = 8
+BLOCK = 512
 
 
 def silu(x):
@@ -44,7 +46,32 @@
 
 
 def encode_kernel(
-    src, grid_lat, feat, dst, w_grid, w_feat, b_enc, w_out, b_out, out, table, even, odd, acc, cnt
+    src_h,
+    grid_h,
+    feat_h,
+    dst_h,
+    w_grid_h,
+    w_feat_h,
+    b_enc_h,
+    w_out_h,
+    b_out_h,
+    out,
+    src,
+    grid_lat,
+    feat,
+    dst,
+    w_grid,
+    w_feat,
+    b_enc,
+    w_out,
+    b_out,
+    table,
+    even,
+    odd,
+    acc,
+    cnt,
+    sems,
+    grid_sems,
 ):
     grid_rows, width = grid_lat.shape
     edges = dst.shape[1]
@@ -52,19 +79,41 @@
     parts = width // LANES
     block = even.shape[0] // parts
     blocks = edges // block
-    rows = 256
-
-    def project(i, carry):
-        p = dot(grid_lat[pl.ds(pl.multiple_of(i * rows, rows), rows), :], w_grid[...]) + b_enc[...]
+    rows = grid_rows // PIECES
+
+    def load(n, source, target):
+        copy = pltpu.make_async_copy(source, target, sems.at[n])
+        copy.start()
+        return copy
+
+    first = [load(0, w_grid_h, w_grid), load(1, b_enc_h, b_enc)]
+    grid_loads = []
+    for i in range(PIECES):
+        piece = pl.ds(i * rows, rows)
+        copy = pltpu.make_async_copy(grid_h.at[piece], grid_lat.at[piece], grid_sems.at[i])
+        copy.start()
+        grid_loads.append(copy)
+    second = [
+        load(2, src_h, src),
+        load(3, feat_h, feat),
+        load(4, dst_h, dst),
+        load(5, w_feat_h, w_feat),
+    ]
+    third = [load(6, w_out_h, w_out), load(7, b_out_h, b_out)]
+
+    acc[...] = jnp.zeros_like(acc)
+    cnt[...] = jnp.zeros_like(cnt)
+    for copy in first:
+        copy.wait()
+    for i in range(PIECES):
+        grid_loads[i].wait()
+        p = dot(grid_lat[i * rows : (i + 1) * rows, :], w_grid[...]) + b_enc[...]
         for j in range(parts):
             table[pl.ds(i * (rows * parts) + j, rows, stride=parts), :] = p[
                 :, j * LANES : (j + 1) * LANES
             ]
-        return carry
-
-    lax.fori_loop(0, grid_rows // rows, project, 0)
-    acc[...] = jnp.zeros_like(acc)
-    cnt[...] = jnp.zeros_like(cnt)
+    for copy in second:
+        copy.wait()
 
     def gather(turn, held):
         base = turn * block
@@ -98,6 +147,8 @@
         return carry
 
     lax.fori_loop(0, blocks // 2, pair, 0)
+    for copy in third:
+        copy.wait()
     count = jnp.sum(cnt[...], axis=1, keepdims=True)
     out[...] = (split_dot(acc[...], w_out[...]) + count * b_out[...]).astype(BF16)
 
@@ -105,21 +156,25 @@
 def encode(grid_lat, feat, src, dst, w_grid, w_feat, b_enc, w_out, b_out, keys):
     width = grid_lat.shape[1]
     parts = width // LANES
-    block = 256
-    vmem = pl.BlockSpec(memory_space=pltpu.VMEM)
+    block = BLOCK
     edges = src.shape[0]
+    operands = (src, grid_lat, feat, dst, w_grid, w_feat, b_enc, w_out, b_out)
     return pl.pallas_call(
         encode_kernel,
         name="encode",
         out_shape=jax.ShapeDtypeStruct((keys, width), BF16),
-        in_specs=[pl.BlockSpec(memory_space=pltpu.SMEM)] + [vmem] * 8,
-        out_specs=vmem,
-        scratch_shapes=[
+        in_specs=[pl.BlockSpec(memory_space=pl.ANY)] * len(operands),
+        out_specs=pl.BlockSpec(memory_space=pltpu.VMEM),
+        scratch_shapes=[pltpu.SMEM(src.shape, src.dtype)]
+        + [pltpu.VMEM(a.shape, a.dtype) for a in operands[1:]]
+        + [
             pltpu.VMEM((grid_lat.shape[0] * parts, LANES), F32),
             pltpu.VMEM((block * parts, LANES), F32),
             pltpu.VMEM((block * parts, LANES), F32),
             pltpu.VMEM((keys, width), F32),
             pltpu.VMEM((keys, LANES), F32),
+            pltpu.SemaphoreType.DMA((8,)),
+            pltpu.SemaphoreType.DMA((PIECES,)),
         ],
         compiler_params=pltpu.CompilerParams(vmem_limit_bytes=VMEM_BYTES),
         cost_estimate=pl.CostEstimate(
@@ -127,16 +182,16 @@
             bytes_accessed=2 * width * (grid_lat.shape[0] + 2 * width),
             transcendentals=edges * width,
         ),
-    )(src, grid_lat, feat, dst, w_grid, w_feat, b_enc, w_out, b_out)
+    )(*operands)
 
 
 def process_kernel(
     peers,
-    part,
-    mesh_lat,
-    mesh_send,
-    senders,
-    receivers,
+    part_h,
+    mesh_lat_h,
+    mesh_send_h,
+    senders_h,
+    receivers_h,
     w_node_self_h,
     w_node_agg_h,
     w_node_out_h,
@@ -146,6 +201,20 @@
     w_proc_self_h,
     w_proc_agg_h,
     w_proc_out_h,
+    b_node_h,
+    b_node_out_h,
+    gain_node_h,
+    b_edge_h,
+    b_edge_out_h,
+    b_proc_h,
+    b_proc_out_h,
+    gain_proc_h,
+    out,
+    part,
+    mesh_lat,
+    mesh_send,
+    senders,
+    receivers,
     b_node,
     b_node_out,
     gain_node,
@@ -154,7 +223,6 @@
     b_proc,
     b_proc_out,
     gain_proc,
-    out,
     weights,
     below,
     above,
@@ -165,6 +233,7 @@
     hits_recv,
     preact,
     weight_sem,
+    small_sem,
     halo_send_sem,
     halo_recv_sem,
     rows_send_sem,
@@ -194,6 +263,26 @@
     loads = [
         pltpu.make_async_copy(ref, weights.at[n], weight_sem.at[n]) for n, ref in enumerate(sources)
     ]
+    small_pairs = (
+        (part_h, part),
+        (mesh_lat_h, mesh_lat),
+        (mesh_send_h, mesh_send),
+        (senders_h, senders),
+        (receivers_h, receivers),
+        (b_node_h, b_node),
+        (b_node_out_h, b_node_out),
+        (gain_node_h, gain_node),
+        (b_edge_h, b_edge),
+        (b_edge_out_h, b_edge_out),
+        (b_proc_h, b_proc),
+        (b_proc_out_h, b_proc_out),
+        (gain_proc_h, gain_proc),
+    )
+    small_loads = [
+        pltpu.make_async_copy(a, b, small_sem.at[n]) for n, (a, b) in enumerate(small_pairs)
+    ]
+    for load in small_loads:
+        load.start()
     for load in loads:
         load.start()
 
@@ -206,6 +295,8 @@
 
     lax.fori_loop(1, peers, greet, 0)
 
+    for load in small_loads:
+        load.wait()
     loads[0].wait()
     latent = mesh_lat[...]
     self_term = dot(latent, weights[0]) + b_node[...]
@@ -355,13 +446,15 @@
     slots = peers * cap
     vmem = pl.BlockSpec(memory_space=pltpu.VMEM)
     hbm = pl.BlockSpec(memory_space=pl.ANY)
+    small = (part, mesh_lat, mesh_send, senders, receivers) + vectors
     return pl.pallas_call(
         functools.partial(process_kernel, peers),
         name="process",
         out_shape=jax.ShapeDtypeStruct((patch, width), BF16),
-        in_specs=[vmem] * 5 + [hbm] * len(mats) + [vmem] * len(vectors),
+        in_specs=[hbm] * (5 + len(mats) + len(vectors)),
         out_specs=vmem,
-        scratch_shapes=[
+        scratch_shapes=[pltpu.VMEM(a.shape, a.dtype) for a in small]
+        + [
             pltpu.VMEM((len(mats), width, width), BF16),
             pltpu.VMEM((patch, width), BF16),
             pltpu.VMEM((patch, width), BF16),
@@ -372,6 +465,7 @@
             pltpu.VMEM((patch, edges), BF16),
             pltpu.VMEM((width, edges), F32),
             pltpu.SemaphoreType.DMA((len(mats),)),
+            pltpu.SemaphoreType.DMA((len(small),)),
             pltpu.SemaphoreType.DMA((2,)),
             pltpu.SemaphoreType.DMA((2,)),
             pltpu.SemaphoreType.DMA,

time: 42 us -> 35.1 us (0.84)
  local copies, waits for them, and re-layouts: 9.44 us -> 2.92 us
    unnamed x60 -> x2, local copies, waits for them, and re-layouts: 9.44 us -> 2.92 us
    pallas_call x1, Pallas kernels: 18.5 us -> 19 us  [process(): pl.pallas_call(functools.partial(process_kernel, peers), name='process',...]
where the time goes in v2:
time: 35.1 us; the launch traced here: 34.9 us
  Pallas kernels  32 us (91%)
  local copies, waits for them, and re-layouts  2.92 us (8%)
    pallas_call x1, Pallas kernels, process(): pl.pallas_call(functools.partial(process_kernel, peers), name='process',...  19 us
    pallas_call x1, Pallas kernels, encode(): pl.pallas_call(encode_kernel, name='encode', out_shape=jax.ShapeDtypeStru...  13 us
    unnamed x2, local copies, waits for them, and re-layouts  2.92 us

profile of v2, /device:TPU:0, one launch (start us, length us, event | category | flops | bytes accessed | tf_op | source)
XLA Modules:
  0.0 34.9 jit_solution(5311704299692366989)
XLA Ops:
  0.0 1.4 %copy.31.mesh_send_h = s32[1,16,8]{2,1,0:T(8,128)} copy(s32[1,16,8]{1,2,0:T(8,128)} %param.35) | data formatting | bytes 1024 | tf_op args[5]
  1.4 13.0 %encode.1.part_h = bf16[384,512]{1,0:T(8,128)(2,1)} custom-call(s32[4096]{0:T(1024)} %src_h.1, bf16[2048,512]{1,0:T(8,128)(2,1)} %grid_h.1, bf16[4,4096]{1,0:T(4,128)(2,1)} %feat_h.1, s32[1,4096]{1,0:T(1,128)} %bitcast.23, bf16[512,512]{1,0:T(8,128)(2,1)} %w_grid_h.1, bf16[4,512]{1,0:T(4,128)(2,1)} %w_feat_h.1, f32[1,512]{1,0:T(1,128)} %bitcast.24, ...), custom_call_target="tpu_custom_call" | custom-call | flops 2684354560 | bytes 3145728 | tf_op jit(solution)/shard_map/encode/pallas_call | solution.py:162
  14.3 19.0 %process.1 = bf16[128,512]{1,0:T(8,128)(2,1)} custom-call(bf16[384,512]{1,0:T(8,128)(2,1)} %encode.1.part_h, bf16[128,512]{1,0:T(8,128)(2,1)} %mesh_lat_h.1, s32[1,16,8]{2,1,0:T(8,128)} %copy.31.mesh_send_h, s32[1,2048]{1,0:T(1,128)} %bitcast.13, s32[1,2048]{1,0:T(1,128)} %bitcast.14, bf16[512,512]{1,0:T(8,128)(2,1)} %w_node_self_h.1, ...), custom_call_target="tpu_custom_call" | custom-call | tf_op jit(solution)/shard_map/process/pallas_call | solution.py:450
  33.4 1.6 %copy.33 = bf16[128,512]{1,0:T(8,128)(2,1)} copy(bf16[128,512]{1,0:T(8,128)(2,1)} %process.1) | data formatting | bytes 262144

commit v3 on v2

--- a/solution.py
+++ b/solution.py
@@ -13,7 +13,7 @@
 MESH_ID = pl.DeviceIdType.MESH
 VMEM_BYTES = 63 * 1024 * 1024 + 512 * 1024
 PIECES = 8
-BLOCK = 512
+BLOCK = 1024
 
 
 def silu(x):
@@ -243,7 +243,7 @@
     me = lax.axis_index("lat")
     patch, width = mesh_lat.shape
     half = width // 2
-    cap = mesh_send.shape[2]
+    cap = mesh_send.shape[1]
     two = 2 * cap
     edges = senders.shape[1]
     slots = peers * cap
@@ -336,7 +336,12 @@
     def _():
         above[...] = jnp.zeros_like(above)
 
-    picks = mesh_send[0].astype(F32)[:, None, :]
+    unit = (
+        lax.broadcasted_iota(jnp.int32, (cap, cap), 0)
+        == lax.broadcasted_iota(jnp.int32, (cap, cap), 1)
+    )
+    unit = jnp.where(unit, 1.0, 0.0).astype(BF16)
+    picks = dot_tn(mesh_send[0].astype(F32).astype(BF16), unit)[:, None, :]
     row = lax.broadcasted_iota(jnp.int32, (peers, two, cap), 1)
     lane = lax.broadcasted_iota(jnp.int32, (peers, two, cap), 2)
     spread = jnp.where(lax.rem(row, cap) == lane, jnp.broadcast_to(picks, row.shape), 0.0)
@@ -441,7 +446,7 @@
 
 def process(peers, part, mesh_lat, mesh_send, senders, receivers, mats, vectors):
     patch, width = mesh_lat.shape
-    cap = mesh_send.shape[2]
+    cap = mesh_send.shape[1]
     edges = senders.shape[1]
     slots = peers * cap
     vmem = pl.BlockSpec(memory_space=pltpu.VMEM)
@@ -532,7 +537,7 @@
         peers,
         part,
         mesh_lat,
-        mesh_send,
+        jnp.swapaxes(mesh_send, 1, 2),
         line(mesh_senders),
         line(mesh_recv),
         (

time: 35.1 us -> 33.3 us (0.949)
  local copies, waits for them, and re-layouts: 2.92 us -> 1.57 us
  Pallas kernels: 32 us -> 31.6 us
    unnamed x2 -> x1, local copies, waits for them, and re-layouts: 2.92 us -> 1.57 us
    pallas_call x1, Pallas kernels: 13 us -> 12.6 us  [encode(): pl.pallas_call(encode_kernel, name='encode', out_shape=jax.ShapeDtypeStru...]
where the time goes in v3:
time: 33.3 us; the launch traced here: 33.2 us
  Pallas kernels  31.6 us (95%)
  local copies, waits for them, and re-layouts  1.57 us (5%)
    pallas_call x1, Pallas kernels, process(): pl.pallas_call(functools.partial(process_kernel, peers), name='process',...  19 us
    pallas_call x1, Pallas kernels, encode(): pl.pallas_call(encode_kernel, name='encode', out_shape=jax.ShapeDtypeStru...  12.6 us
    unnamed x1, local copies, waits for them, and re-layouts  1.57 us

profile of v3, /device:TPU:0, one launch (start us, length us, event | category | flops | bytes accessed | tf_op | source)
XLA Modules:
  0.0 33.2 jit_solution(8030447369451611411)
XLA Ops:
  0.0 12.6 %encode.1.part_h = bf16[384,512]{1,0:T(8,128)(2,1)} custom-call(s32[4096]{0:T(1024)} %src_h.1, bf16[2048,512]{1,0:T(8,128)(2,1)} %grid_h.1, bf16[4,4096]{1,0:T(4,128)(2,1)} %feat_h.1, s32[1,4096]{1,0:T(1,128)} %bitcast.25, bf16[512,512]{1,0:T(8,128)(2,1)} %w_grid_h.1, bf16[4,512]{1,0:T(4,128)(2,1)} %w_feat_h.1, f32[1,512]{1,0:T(1,128)} %bitcast.26, ...), custom_call_target="tpu_custom_call" | custom-call | flops 2684354560 | bytes 3145728 | tf_op jit(solution)/shard_map/encode/pallas_call | solution.py:162
  12.6 19.0 %process.1 = bf16[128,512]{1,0:T(8,128)(2,1)} custom-call(bf16[384,512]{1,0:T(8,128)(2,1)} %encode.1.part_h, bf16[128,512]{1,0:T(8,128)(2,1)} %mesh_lat_h.1, s32[1,8,16]{2,1,0:T(8,128)} %bitcast.16, s32[1,2048]{1,0:T(1,128)} %bitcast.14, s32[1,2048]{1,0:T(1,128)} %bitcast.15, bf16[512,512]{1,0:T(8,128)(2,1)} %w_node_self_h.1, bf16[512,512]{1,0:T(8,128)(2,1)} %w_node_agg_h.1, ...), custom_call_target="tpu_custom_call" | custom-call | tf_op jit(solution)/shard_map/process/pallas_call | solution.py:455
  31.6 1.6 %copy.32 = bf16[128,512]{1,0:T(8,128)(2,1)} copy(bf16[128,512]{1,0:T(8,128)(2,1)} %process.1) | data formatting | bytes 262144
